TPU v7x, 512 devices: a whole 4x4x16 slice. The times are simulated.
512 devices in a mesh: seq: 128 (over x, y, z_lo), head: 4 (over z_hi, core).
Axes of the slice: x: 4, y: 4, z: 16 (z_hi: 2, z_lo: 8; z = z_hi * 8 + z_lo), core: 2. Of those that a mesh axis runs over, the one named last changes fastest.
Arguments:
- tile_embed: bfloat16 [131072, 768], P('seq'), may hold values from -82 to 82
- tile_counts: int32 [2], replicated, may hold values from 32769 to 65536, as said below
- w_qkv: bfloat16 [3, 768, 768], P(None, None, 'head'), may hold values from -0.21875 to 0.21875
- w_out: bfloat16 [768, 768], replicated, may hold values from -0.21875 to 0.21875
Outputs:
- encoded: bfloat16 [131072, 768], P('seq', 'head')
Inputs may be any that keep to these rules, and one draw needn't show every extreme that they name: `tile_counts`: one of the two slides holds all 65536 tiles.
All inputs are finite; a program needn't handle non-finite values.
Results may differ from a plain program's by a relative error of at most 0.007.
The roundings to bfloat16 on the way count: a program that leaves them out, or rounds other values in their place, can miss the bound.
Values may be sent and summed in bfloat16 or wider, within the bound.
A program may use at most 64 MiB of HBM per device.

v0:
```python
import jax
import jax.numpy as jnp
from jax import lax
from jax.sharding import PartitionSpec as P

HD = 48


def swapped(shard, axis, bit):
    return lax.ppermute(shard, axis, [(i, i ^ 1 << bit) for i in range(lax.axis_size(axis))])


def valid_rows(position, tile_counts, half_len):
    slide_id = position // half_len
    row_limit = jnp.where(slide_id == 0, tile_counts[0], tile_counts[1])
    return position - slide_id * half_len < row_limit


def head_terms(query_rows, key_rows, value_rows, key_ok):
    scores = jnp.dot(query_rows, key_rows.T, preferred_element_type=jnp.float32) * query_rows.shape[
        1
    ] ** (-0.5)
    masked = jnp.where(key_ok[None, :], scores, -1e30)
    row_max = jnp.max(masked, axis=1)
    weights = jnp.where(key_ok[None, :], jnp.exp(scores - row_max[:, None]), 0.0)
    denom_sum = jnp.sum(weights, axis=1)
    summed = jnp.dot(weights.astype(jnp.bfloat16), value_rows, preferred_element_type=jnp.float32)
    return (row_max, denom_sum, summed)


def merge_state(carried, row_max, level_den, level_out):
    best, denom_sum, summed = carried
    new_best = jnp.maximum(best, row_max)
    old_wt = jnp.exp(best - new_best)
    new_wt = jnp.exp(row_max - new_best)
    return (
        new_best,
        denom_sum * old_wt + level_den * new_wt,
        summed * old_wt[..., None] + level_out * new_wt[..., None],
    )


def all_heads(operands):

    def per_head(items):
        return head_terms(items[0], items[1], items[2], items[3])

    return lax.map(per_head, operands)


def on_device(tile_embed, tile_counts, w_qkv, w_out):
    row_count = tile_embed.shape[0]
    seq_devs = lax.axis_size("seq")
    device_idx = lax.axis_index("seq")
    local_width = w_qkv.shape[2]
    local_heads = local_width // HD
    half_len = row_count * seq_devs // 2
    top_group = min(16, seq_devs // 2)
    levels = top_group.bit_length()
    projected = jnp.einsum(
        "rd,cde->cre", tile_embed, w_qkv, preferred_element_type=jnp.float32
    ).astype(jnp.bfloat16)
    queries = projected[0].reshape(row_count, local_heads, HD).transpose(1, 0, 2)
    key_rows = projected[1].reshape(row_count, local_heads, HD).transpose(1, 0, 2)
    value_rows = projected[2].reshape(row_count, local_heads, HD).transpose(1, 0, 2)
    head_ids = lax.axis_index("head") * local_heads + jnp.arange(local_heads, dtype=jnp.int32)
    row_index = jnp.arange(row_count, dtype=jnp.int32)
    query_valid = valid_rows(device_idx * row_count + row_index, tile_counts, half_len)
    carried = (
        jnp.full((local_heads, row_count), -1e30, jnp.float32),
        jnp.zeros((local_heads, row_count), jnp.float32),
        jnp.zeros((local_heads, row_count, HD), jnp.float32),
    )
    for tier_idx in range(levels):
        stride = 2**tier_idx
        if tier_idx > 0:
            parity = head_ids // (stride // 2) % 2
            select_idx = parity[:, None, None, None]
            own_keys = jnp.take_along_axis(
                key_rows.reshape(local_heads, row_count // 2, 2, HD), select_idx, axis=2
            )[:, :, 0]
            own_values = jnp.take_along_axis(
                value_rows.reshape(local_heads, row_count // 2, 2, HD), select_idx, axis=2
            )[:, :, 0]
            partner = swapped(jnp.stack((own_keys, own_values)), "seq", tier_idx - 1)
            low_half = device_idx // (stride // 2) % 2 == 0
            key_rows = jnp.where(
                low_half,
                jnp.concatenate((own_keys, partner[0]), axis=1),
                jnp.concatenate((partner[0], own_keys), axis=1),
            )
            value_rows = jnp.where(
                low_half,
                jnp.concatenate((own_values, partner[1]), axis=1),
                jnp.concatenate((partner[1], own_values), axis=1),
            )
        offsets = head_ids % stride
        group_start = device_idx // stride * stride
        key_pos = group_start * row_count + offsets[:, None] + row_index[None, :] * stride
        key_ok = valid_rows(key_pos, tile_counts, half_len)
        query_sel = jnp.take_along_axis(
            queries.reshape(local_heads, row_count // stride, stride, HD),
            offsets[:, None, None, None],
            axis=2,
        )[:, :, 0]
        operands = (query_sel, key_rows, value_rows, key_ok)
        row_max, level_den, level_out = all_heads(operands)
        chosen = jnp.arange(stride, dtype=jnp.int32)[None, :] == offsets[:, None]
        max_full = jnp.where(chosen[:, None, :], row_max[:, :, None], -1e30).reshape(
            local_heads, row_count
        )
        den_full = jnp.where(chosen[:, None, :], level_den[:, :, None], 0.0).reshape(
            local_heads, row_count
        )
        out_full = jnp.where(chosen[:, None, :, None], level_out[:, :, None, :], 0.0).reshape(
            local_heads, row_count, HD
        )
        carried = merge_state(carried, max_full, den_full, out_full)
    safe_den = jnp.where(query_valid[None, :], carried[1], 1.0)
    attn = jnp.where(query_valid[None, :, None], carried[2] / safe_den[..., None], 0.0).astype(
        jnp.bfloat16
    )
    attn_rows = attn.transpose(1, 0, 2).reshape(row_count, local_width)
    head_idx = lax.axis_index("head")
    partial_sum = jnp.dot(
        attn_rows,
        lax.dynamic_slice_in_dim(w_out, head_idx * local_width, local_width, 0),
        preferred_element_type=jnp.float32,
    )
    encoded = lax.psum_scatter(partial_sum, "head", scatter_dimension=1, tiled=True)
    return encoded.astype(jnp.bfloat16)


def solution(mesh):
    in_specs = (P("seq", None), P(), P(None, None, "head"), P())
    out_specs = P("seq", "head")
    return jax.shard_map(
        on_device, mesh=mesh, in_specs=in_specs, out_specs=out_specs, check_vma=False
    )
```

profile of v0, /device:TPU:1, one launch (start us, length us, event | category | flops | bytes accessed | tf_op | source)
XLA Modules:
  0.0 375.7 jit_solution(11885341834821720907)
XLA Ops:
  7.9 2.3 fusion.101
  11.1 1.5 copy.47
  12.6 2.0 copy.54
  15.0 1.9 copy.53
  17.0 1.6 gather_fusion.6
  18.5 1.6 gather_fusion.5
  20.6 1.8 copy.52
  22.4 2.3 gather_fusion.4
  24.7 1.9 fusion.108
  27.3 4.4 %collective-permute-start = (bf16[2,4,512,48]{2,3,1,0:T(8,128)(2,1)}, bf16[2,4,512,48]{2,3,1,0:T(8,128)(2,1)}, u32[]{:S(2)}, u32[]{:S(2)}) collective-permute-start(bf16[2,4,512,48]{2,3,1,0:T(8,128)(2,1)} %pad_maximum_fusion), channel_id=1, source_target_pairs={{0,4},{4,0},{8,12},{12,8},{16,20},{20,16},{24,28},{28,24},{32,36},... | collective-permute-start | bytes 1179656 | tf_op jit(solution)/shard_map/ppermute | solution.py:10
  37.6 26.1 %while.75 = (s32[]{:T(128)}, f32[4,1024]{1,0:T(4,128)S(1)}, f32[4,1024]{1,0:T(4,128)}, f32[4,1024,48]{1,2,0:T(8,128)}, pred[4,1024]{1,0:T(4,128)(4,1)S(1)}, /*in...) while((s32[]{:T(128)}, f32[4,1024]{1,0:T(4,128)S(1)}, ...), condition=%wide.region_3.4_spmd.clone, body=%wide.region_0.3_spmd.sunk.clone | while | flops 212858880 | bytes 13442153 | solution.py:48
  37.6 1.7 select_reduce_fusion.15
  40.2 2.5 fusion.219
  42.7 1.3 dynamic_update_slice.92
  44.1 1.7 select_reduce_fusion.15
  46.7 2.5 fusion.219
  50.6 1.7 select_reduce_fusion.15
  53.2 2.5 fusion.219
  57.2 1.7 select_reduce_fusion.15
  59.7 2.5 fusion.219
  63.7 1.3 copy.72
  66.0 1.9 fusion.137
  68.0 1.9 fusion.139
  69.9 1.6 gather_fusion.2
  72.8 2.6 fusion.135
  75.5 1.8 select_compare_fusion.1
  81.7 3.1 copy.50
  88.7 1.9 maximum_select_fusion
  90.6 1.5 copy.56
  92.1 1.8 copy.64
  94.7 1.6 gather_fusion.7
  97.2 5.1 %collective-permute-start.1 = (bf16[2,4,512,48]{2,3,1,0:T(8,128)(2,1)S(1)}, bf16[2,4,512,48]{2,3,1,0:T(8,128)(2,1)}, u32[]{:S(2)}, u32[]{:S(2)}) collective-permute-start(bf16[2,4,512,48]{2,3,1,0:T(8,128)(2,1)S(1)} %pad_maximum_fusion.1), channel_id=1, source_target_pairs={{0,8},{4,12},{8,0},{12,4},{16,24},{20,28},{24,16},{28,20},{32,40},... | collective-permute-start | bytes 1179656 | tf_op jit(solution)/shard_map/ppermute | solution.py:10
  102.3 17.3 %while.76 = (s32[]{:T(128)}, f32[4,512]{1,0:T(4,128)S(1)}, f32[4,512]{1,0:T(4,128)S(1)}, f32[4,512,48]{1,2,0:T(8,128)}, pred[4,1024]{1,0:T(4,128)(4,1)S(1)}, /*i...) while((s32[]{:T(128)}, f32[4,512]{1,0:T(4,128)S(1)}, ...), condition=%wide.region_7.9_spmd.clone, body=%wide.region_4.8_spmd.sunk.clone | while | flops 106429440 | bytes 6986857 | solution.py:48
  102.4 1.4 select_reduce_fusion.16
  104.3 2.2 fusion.223
  106.7 1.4 select_reduce_fusion.16
  108.7 2.2 fusion.223
  111.0 1.4 select_reduce_fusion.16
  113.0 2.2 fusion.223
  115.4 1.4 select_reduce_fusion.16
  117.3 2.2 fusion.223
  121.9 2.3 copy.60
  126.6 1.9 maximum_select_fusion.3
  128.5 2.3 copy.69
  130.8 3.5 copy.76
  135.2 1.7 gather_fusion.10
  136.9 1.5 fusion.116
  138.4 8.8 %collective-permute-start.2 = (bf16[2,4,512,48]{2,3,1,0:T(8,128)(2,1)S(1)}, bf16[2,4,512,48]{2,3,1,0:T(8,128)(2,1)}, u32[]{:S(2)}, u32[]{:S(2)}) collective-permute-start(bf16[2,4,512,48]{2,3,1,0:T(8,128)(2,1)S(1)} %pad_maximum_fusion.2), channel_id=1, source_target_pairs={{0,16},{4,20},{8,24},{12,28},{16,0},{20,4},{24,8},{28,12},{32,48},... | collective-permute-start | bytes 1179656 | tf_op jit(solution)/shard_map/ppermute | solution.py:10
  147.2 8.8 %while.77 = (s32[]{:T(128)}, f32[4,256]{1,0:T(4,128)S(1)}, f32[4,256]{1,0:T(4,128)S(1)}, f32[4,256,48]{1,2,0:T(8,128)S(1)}, pred[4,1024]{1,0:T(4,128)(4,1)S(1)},...) while((s32[]{:T(128)}, f32[4,256]{1,0:T(4,128)S(1)}, ...), condition=%wide.region_11.13_spmd.clone, body=%wide.region_8.12_spmd.sunk.clone | while | flops 52690432 | bytes 3759209 | solution.py:48
  158.7 22.9 %collective-permute-done.2 = bf16[2,4,512,48]{2,3,1,0:T(8,128)(2,1)} collective-permute-done((bf16[2,4,512,48]{2,3,1,0:T(8,128)(2,1)S(1)}, bf16[2,4,512,48]{2,3,1,0:T(8,128)(2,1)}, u32[]{:S(2)}, u32[]{:S(2)}) %collective-permute-start.2) | collective-permute-done | bytes 393248 | tf_op jit(solution)/shard_map/ppermute | solution.py:10
  184.0 1.9 maximum_select_fusion.4
  185.8 2.3 copy.78
  188.2 3.5 copy.84
  192.3 1.6 gather_fusion.11
  195.5 3.4 collective-permute-start.3
  199.0 10.2 %while.78 = (s32[]{:T(128)}, f32[4,128]{1,0:T(4,128)S(1)}, f32[4,128]{1,0:T(4,128)S(1)}, f32[4,128,48]{1,2,0:T(8,128)}, pred[4,1024]{1,0:T(4,128)(4,1)S(1)}, /*i...) while((s32[]{:T(128)}, f32[4,128]{1,0:T(4,128)S(1)}, ...), condition=%wide.region_15.17_spmd.clone, body=%wide.region_12.16_spmd.sunk.clone | while | flops 26345216 | bytes 2145385 | solution.py:48
  213.3 11.8 %while.79 = (s32[]{:T(128)}, f32[4,64]{1,0:T(4,128)S(1)}, f32[4,64]{1,0:T(4,128)}, f32[4,64,48]{1,2,0:T(8,128)S(1)}, pred[4,1024]{1,0:T(4,128)(4,1)S(1)}, /*inde...) while((s32[]{:T(128)}, f32[4,64]{1,0:T(4,128)S(1)}, ...), condition=%wide.region_19.21_spmd.clone, body=%wide.region_16.20_spmd.sunk.clone | while | flops 13172610 | bytes 1029481 | solution.py:48
  225.8 1.5 broadcast_in_dim.607
  228.3 1.4 broadcast_in_dim.619
  229.7 1.6 broadcast_in_dim.620
  234.6 9.0 %fusion.95 = bf16[4,1024,48]{2,1,0:T(8,128)(2,1)S(1)} fusion(f32[4,1024,48]{2,1,0:T(8,128)S(1)} %bitcast.437, f32[4,1024,48]{2,1,0:T(8,128)S(1)} %bitcast.438, f32[4,1024,48]{2,1,0:T(8,128)S(1)} %copy-done.2, f32[4,1024]{1,0:T(4,128)S(1)} %get-tuple-element.401, f32[4,1024]{1,0:T(4,128)S(1)} %get-tuple-element.409, f32[4,64,48]{2,1,0:T(8,128)S(1)} %copy.90, ...), kind=kLoop, calls=%fused_computation.123 | loop fusion | flops 4128768 | bytes 3097600 | tf_op jit(solution)/shard_map/convert_element_type | solution.py:120
  243.9 3.2 fusion.104
  247.2 119.7 %reduce-scatter.2.cloned.1.call-done = f32[1024,192]{0,1:T(8,128)} async-done(((f32[1024,768]{0,1:T(8,128)}), f32[1024,192]{0,1:T(8,128)}) %reduce-scatter.2.cloned.1.call-update) | async-done | bytes 786448 | tf_op jit(solution)/shard_map/reduce_scatter | solution.py:130
  366.9 1.9 convert_element_type.30
  (316 shorter events, 85.1 us)
Async XLA Ops:
  6.5 1.4 copy-start
  6.5 360.3 %reduce-scatter.2.cloned.1.call-start = ((), (), s32[]{:S(2)}) async-start(), calls=%async_computation.1 | async-start | bytes 3932160 | tf_op jit(solution)/shard_map/reduce_scatter | solution.py:130
  12.6 2.0 copy-start.4
  15.0 5.1 %copy-start.1 = (bf16[1024,4,48]{2,0,1:T(8,128)(2,1)}, bf16[1024,4,48]{2,0,1:T(8,128)(2,1)S(1)}, u32[]{:S(2)}) copy-start(bf16[1024,4,48]{2,0,1:T(8,128)(2,1)S(1)} %copy.46) | copy-start | bytes 1179652
  22.4 10.5 %copy-start.43 = (s32[2]{0:T(128)S(1)}, s32[2]{0:T(128)}, u32[]{:S(2)}) copy-start(s32[2]{0:T(128)} %param.17) | copy-start | bytes 28
  27.3 58.8 %collective-permute-start = (bf16[2,4,512,48]{2,3,1,0:T(8,128)(2,1)}, bf16[2,4,512,48]{2,3,1,0:T(8,128)(2,1)}, u32[]{:S(2)}, u32[]{:S(2)}) collective-permute-start(bf16[2,4,512,48]{2,3,1,0:T(8,128)(2,1)} %pad_maximum_fusion), channel_id=1, source_target_pairs={{0,4},{4,0},{8,12},{12,8},{16,20},{20,16},{24,28},{28,24},{32,36},... | collective-permute-start | bytes 1179656 | tf_op jit(solution)/shard_map/ppermute | solution.py:10
  63.7 4.3 %copy-start.29 = (f32[4,1024]{1,0:T(4,128)}, f32[4,1024]{1,0:T(4,128)S(1)}, u32[]{:S(2)}) copy-start(f32[4,1024]{1,0:T(4,128)S(1)} %get-tuple-element.226) | copy-start | bytes 49156
  81.2 4.8 %copy-start.45 = (pred[4]{0:T(512)(128)(4,1)S(1)}, pred[4]{0:T(512)(128)(4,1)}, u32[]{:S(2)}) copy-start(pred[4]{0:T(512)(128)(4,1)} %get-tuple-element.479) | copy-start | bytes 16
  81.7 5.4 %copy-start.7 = (bf16[4,512,48]{1,2,0:T(8,128)(2,1)S(1)}, bf16[4,512,48]{1,2,0:T(8,128)(2,1)}, u32[]{:S(2)}) copy-start(bf16[4,512,48]{1,2,0:T(8,128)(2,1)} %get-tuple-element.467) | copy-start | bytes 589828
  87.7 1.0 copy-start.5
  90.6 4.1 %copy-start.33 = (s32[4]{0:T(128)S(1)}, s32[4]{0:T(128)}, u32[]{:S(2)}) copy-start(s32[4]{0:T(128)} %or_bitcast_fusion.2) | copy-start | bytes 52
  92.1 4.2 %copy-start.44 = (pred[4]{0:T(512)(128)(4,1)S(1)}, pred[4]{0:T(512)(128)(4,1)}, u32[]{:S(2)}) copy-start(pred[4]{0:T(512)(128)(4,1)} %get-tuple-element.474) | copy-start | bytes 16
  93.9 8.4 %copy-start.19 = (pred[4,1024]{1,0:T(4,128)(4,1)S(1)}, pred[4,1024]{1,0:T(4,128)(4,1)}, u32[]{:S(2)}) copy-start(pred[4,1024]{1,0:T(4,128)(4,1)} %get-tuple-element.888) | copy-start | bytes 12292
  93.9 8.4 %copy-start.35 = (f32[4,512]{1,0:T(4,128)S(1)}, f32[4,512]{1,0:T(4,128)}, u32[]{:S(2)}) copy-start(f32[4,512]{1,0:T(4,128)} %custom-call.37) | copy-start | bytes 24580
  93.9 8.4 %copy-start.36 = (f32[4,512]{1,0:T(4,128)S(1)}, f32[4,512]{1,0:T(4,128)}, u32[]{:S(2)}) copy-start(f32[4,512]{1,0:T(4,128)} %custom-call.36) | copy-start | bytes 24580
  97.2 27.0 %collective-permute-start.1 = (bf16[2,4,512,48]{2,3,1,0:T(8,128)(2,1)S(1)}, bf16[2,4,512,48]{2,3,1,0:T(8,128)(2,1)}, u32[]{:S(2)}, u32[]{:S(2)}) collective-permute-start(bf16[2,4,512,48]{2,3,1,0:T(8,128)(2,1)S(1)} %pad_maximum_fusion.1), channel_id=1, source_target_pairs={{0,8},{4,12},{8,0},{12,4},{16,24},{20,28},{24,16},{28,20},{32,40},... | collective-permute-start | bytes 1179656 | tf_op jit(solution)/shard_map/ppermute | solution.py:10
  120.0 5.3 %copy-start.9 = (bf16[4,512,48]{1,2,0:T(8,128)(2,1)S(1)}, bf16[4,512,48]{1,2,0:T(8,128)(2,1)}, u32[]{:S(2)}) copy-start(bf16[4,512,48]{1,2,0:T(8,128)(2,1)} %get-tuple-element.464) | copy-start | bytes 589828
  134.3 12.9 %copy-start.12 = (f32[4,256,48]{1,2,0:T(8,128)S(1)}, f32[4,256,48]{1,2,0:T(8,128)}, u32[]{:S(2)}) copy-start(f32[4,256,48]{1,2,0:T(8,128)} %custom-call.41) | copy-start | bytes 589828
  135.1 12.1 %copy-start.17 = (pred[4,1024]{1,0:T(4,128)(4,1)S(1)}, pred[4,1024]{1,0:T(4,128)(4,1)}, u32[]{:S(2)}) copy-start(pred[4,1024]{1,0:T(4,128)(4,1)} %fusion.137) | copy-start | bytes 12292
  135.1 12.1 %copy-start.37 = (f32[4,256]{1,0:T(4,128)S(1)}, f32[4,256]{1,0:T(4,128)}, u32[]{:S(2)}) copy-start(f32[4,256]{1,0:T(4,128)} %custom-call.40) | copy-start | bytes 12292
  135.2 12.1 %copy-start.38 = (f32[4,256]{1,0:T(4,128)S(1)}, f32[4,256]{1,0:T(4,128)}, u32[]{:S(2)}) copy-start(f32[4,256]{1,0:T(4,128)} %custom-call.39) | copy-start | bytes 12292
  138.4 43.2 %collective-permute-start.2 = (bf16[2,4,512,48]{2,3,1,0:T(8,128)(2,1)S(1)}, bf16[2,4,512,48]{2,3,1,0:T(8,128)(2,1)}, u32[]{:S(2)}, u32[]{:S(2)}) collective-permute-start(bf16[2,4,512,48]{2,3,1,0:T(8,128)(2,1)S(1)} %pad_maximum_fusion.2), channel_id=1, source_target_pairs={{0,16},{4,20},{8,24},{12,28},{16,0},{20,4},{24,8},{28,12},{32,48},... | collective-permute-start | bytes 1179656 | tf_op jit(solution)/shard_map/ppermute | solution.py:10
  156.0 26.6 %copy-start.11 = (bf16[4,512,48]{1,2,0:T(8,128)(2,1)S(1)}, bf16[4,512,48]{1,2,0:T(8,128)(2,1)}, u32[]{:S(2)}) copy-start(bf16[4,512,48]{1,2,0:T(8,128)(2,1)} %get-tuple-element.461) | copy-start | bytes 589828
  157.6 54.0 %copy-start.14 = (f32[4,1024]{1,0:T(4,128)}, f32[4,1024]{1,0:T(4,128)S(1)}, u32[]{:S(2)}) copy-start(f32[4,1024]{1,0:T(4,128)S(1)} %broadcast_in_dim.588) | copy-start | bytes 49156
  184.0 7.7 %copy-start.32 = (s32[4]{0:T(128)S(1)}, s32[4]{0:T(128)}, u32[]{:S(2)}) copy-start(s32[4]{0:T(128)} %or_bitcast_fusion) | copy-start | bytes 52
  188.2 5.6 %copy-start.46 = (pred[4]{0:T(512)(128)(4,1)S(1)}, pred[4]{0:T(512)(128)(4,1)}, u32[]{:S(2)}) copy-start(pred[4]{0:T(512)(128)(4,1)} %get-tuple-element.472) | copy-start | bytes 16
  191.7 7.3 %copy-start.16 = (pred[4,1024]{1,0:T(4,128)(4,1)S(1)}, pred[4,1024]{1,0:T(4,128)(4,1)}, u32[]{:S(2)}) copy-start(pred[4,1024]{1,0:T(4,128)(4,1)} %fusion.139) | copy-start | bytes 12292
  191.7 7.3 %copy-start.41 = (f32[4,128]{1,0:T(4,128)S(1)}, f32[4,128]{1,0:T(4,128)}, u32[]{:S(2)}) copy-start(f32[4,128]{1,0:T(4,128)} %custom-call.43) | copy-start | bytes 6148
  191.7 7.3 %copy-start.42 = (f32[4,128]{1,0:T(4,128)S(1)}, f32[4,128]{1,0:T(4,128)}, u32[]{:S(2)}) copy-start(f32[4,128]{1,0:T(4,128)} %custom-call.42) | copy-start | bytes 6148
  195.5 16.7 %collective-permute-start.3 = (bf16[2,4,512,48]{2,3,1,0:T(8,128)(2,1)}, bf16[2,4,512,48]{2,3,1,0:T(8,128)(2,1)S(1)}, u32[]{:S(2)}, u32[]{:S(2)}) collective-permute-start(bf16[2,4,512,48]{2,3,1,0:T(8,128)(2,1)} %pad_maximum_fusion.3), channel_id=1, source_target_pairs={{0,32},{4,36},{8,40},{12,44},{16,48},{20,52},{24,56},{28,60},{32,0... | collective-permute-start | bytes 1179656 | tf_op jit(solution)/shard_map/ppermute | solution.py:10
  199.0 12.6 %copy-start.13 = (f32[4,1024]{1,0:T(4,128)S(1)}, f32[4,1024]{1,0:T(4,128)}, u32[]{:S(2)}) copy-start(f32[4,1024]{1,0:T(4,128)} %copy.59) | copy-start | bytes 49156
  199.0 12.6 %copy-start.21 = (pred[4,1024]{1,0:T(4,128)(4,1)S(1)}, pred[4,1024]{1,0:T(4,128)(4,1)}, u32[]{:S(2)}) copy-start(pred[4,1024]{1,0:T(4,128)(4,1)} %broadcast_in_dim.575) | copy-start | bytes 12292
  199.0 12.6 %copy-start.25 = (pred[4,1024]{1,0:T(4,128)(4,1)S(1)}, pred[4,1024]{1,0:T(4,128)(4,1)}, u32[]{:S(2)}) copy-start(pred[4,1024]{1,0:T(4,128)(4,1)} %broadcast_in_dim.593) | copy-start | bytes 12292
  199.0 12.6 %copy-start.27 = (pred[4,1024]{1,0:T(4,128)(4,1)S(1)}, pred[4,1024]{1,0:T(4,128)(4,1)}, u32[]{:S(2)}) copy-start(pred[4,1024]{1,0:T(4,128)(4,1)} %broadcast_in_dim.583) | copy-start | bytes 12292
  199.0 12.6 %copy-start.30 = (f32[4,1024]{1,0:T(4,128)S(1)}, f32[4,1024]{1,0:T(4,128)}, u32[]{:S(2)}) copy-start(f32[4,1024]{1,0:T(4,128)} %copy-done.29) | copy-start | bytes 49156
  209.2 3.0 copy-start.10
  209.2 3.9 %copy-start.8 = (bf16[4,512,48]{1,2,0:T(8,128)(2,1)S(1)}, bf16[4,512,48]{1,2,0:T(8,128)(2,1)}, u32[]{:S(2)}) copy-start(bf16[4,512,48]{1,2,0:T(8,128)(2,1)} %get-tuple-element.459) | copy-start | bytes 589828
  209.2 4.0 %copy-start.18 = (pred[4,1024]{1,0:T(4,128)(4,1)S(1)}, pred[4,1024]{1,0:T(4,128)(4,1)}, u32[]{:S(2)}) copy-start(pred[4,1024]{1,0:T(4,128)(4,1)} %get-tuple-element.936) | copy-start | bytes 12292
  209.2 4.0 %copy-start.20 = (f32[4,64,48]{1,2,0:T(8,128)S(1)}, f32[4,64,48]{1,2,0:T(8,128)}, u32[]{:S(2)}) copy-start(f32[4,64,48]{1,2,0:T(8,128)} %custom-call.47) | copy-start | bytes 147460
  209.3 4.0 %copy-start.39 = (f32[4,64]{1,0:T(4,128)S(1)}, f32[4,64]{1,0:T(4,128)}, u32[]{:S(2)}) copy-start(f32[4,64]{1,0:T(4,128)} %custom-call.45) | copy-start | bytes 3076
  210.6 2.6 copy-start.15
  213.3 19.0 %copy-start.3 = (f32[4,512,48]{2,1,0:T(8,128)S(1)}, f32[4,512,48]{2,1,0:T(8,128)}, u32[]{:S(2)}) copy-start(f32[4,512,48]{2,1,0:T(8,128)} %copy.60) | copy-start | bytes 1179652
  225.1 0.6 copy-start.40
  225.8 7.3 %copy-start.6 = (f32[4,256,48]{2,1,0:T(8,128)S(1)}, f32[4,256,48]{2,1,0:T(8,128)}, u32[]{:S(2)}) copy-start(f32[4,256,48]{2,1,0:T(8,128)} %copy.70) | copy-start | bytes 589828
  233.0 1.6 copy-start.2
  233.0 1.6 copy-start.22
  233.0 1.6 copy-start.23
  233.0 1.6 copy-start.24
  233.0 1.6 copy-start.26
  233.0 1.6 copy-start.28
  233.0 1.6 copy-start.31
  233.1 1.6 copy-start.34
Sparse Core Ops, SparseCore 0:
  247.3 119.5 reduce-scatter.1
where the time goes:
time: 378 us; the launch traced here: 376 us
  waiting for transfers between devices  143 us (38%)
  local copies, waits for them, and re-layouts  87.9 us (23%)
  matrix products  58.4 us (15%)
  other arithmetic  50.1 us (13%)
  starting transfers between devices  21.7 us (6%)
  between operations  14.6 us (4%)
    reduce_scatter x1, waiting for transfers between devices, on_device(): lax.psum_scatter(partial_sum, 'head', scatter_dimension=1, tiled=True)  120 us
    dot_general x20, matrix products, head_terms(): jnp.dot(weights.astype(jnp.bfloat16), value_rows, preferred_element_type=...  32.6 us
    ppermute x4, waiting for transfers between devices, swapped(): lax.ppermute(shard, axis, [(i, i ^ 1 << bit) for i in range(lax.axis_size...  22.9 us
    ppermute x4, starting transfers between devices, swapped(): lax.ppermute(shard, axis, [(i, i ^ 1 << bit) for i in range(lax.axis_size...  21.7 us
    dot_general x20, matrix products, head_terms(): jnp.dot(query_rows, key_rows.T, preferred_element_type=jnp.float32)  20.3 us
    while x13, local copies, waits for them, and re-layouts, all_heads(): return lax.map(per_head, operands)  15.5 us
    dynamic_update_slice x40, local copies, waits for them, and re-layouts, all_heads(): return lax.map(per_head, operands)  11.4 us
    lt x5, other arithmetic, valid_rows(): return position - slide_id * half_len < row_limit  9.59 us
  transfers between devices with their start and end apart: 5, of which 2 were waited for; matrix products, arithmetic and copies ran while one was open for 27% of the time, Pallas kernels for 0%

commit v1 on v0

v1 whole, which is shorter than its diff:
```python
import functools
import math

import jax
import jax.numpy as jnp
from jax import lax
from jax.experimental import pallas as pl
from jax.experimental.pallas import tpu as pltpu
from jax.sharding import PartitionSpec as P

HD = 48
ROWS = 1024
D = 768
HALF = 64
CORD = [int(f"{j:04b}"[::-1], 2) for j in range(16)]
JOF = [CORD.index(c) for c in range(16)]
NEG = -1e30
SCALE = math.log2(math.e) / math.sqrt(HD)
MESH = pl.DeviceIdType.MESH
TILE = 256

R1, CR, FW = 8, 12, 16


def kernel(x_ref, cnt_ref, w_ref, wo_ref, o_ref, xp, wr, y, kvb, r4, qp, ka, va, acc, mx, posl, nb, att, eb,
           ss, rs, w1, w2s, w2r, cs):
    f32, bf16, i32 = jnp.float32, jnp.bfloat16, jnp.int32
    s = lax.axis_index("seq")
    hd = lax.axis_index("head")
    px, py, zl = s // 32, s // 8 % 4, s % 8
    zh, cc = hd // 2, hd % 2
    z = zh * 8 + zl
    xy = px * 4 + py
    p4 = zl % 4
    pair = p4 // 2
    inner = (p4 + 1) // 2 % 2
    za = z + 1 - 2 * (z % 2)
    zb = (z + 15 + 2 * (z % 2)) % 16
    zm = 15 - z
    ub = CR + (FW - CR) * (1 - inner)
    wb = FW - (FW - CR) * (1 - inner)

    def dev(xy_, z_, c_):
        return (xy_ * 8 + z_ % 8, z_ // 8 * 2 + c_)

    dev_a, dev_b, dev_m, dev_c = dev(xy, za, cc), dev(xy, zb, cc), dev(xy, zm, cc), dev(xy, z, 1 - cc)
    dev_y = dev(xy + 1 - 2 * (py % 2), z, cc)

    bar = pltpu.get_barrier_semaphore()
    for d in (dev_a, dev_b, dev_m, dev_c):
        pl.semaphore_signal(bar, inc=1, device_id=d, device_id_type=MESH)

    @pl.loop(1, 16)
    def _(k):
        pl.semaphore_signal(bar, inc=1, device_id=dev((xy + k) % 16, z, cc), device_id_type=MESH)

    def rcopy(src, dst, ssem, rsem, d):
        return pltpu.make_async_remote_copy(
            src_ref=src, dst_ref=dst, send_sem=ssem, recv_sem=rsem, device_id=d, device_id_type=MESH
        )

    def send_l1(g, i):
        lo, n = ((0, 1), (1, 1), (2, 2))[i]
        return rcopy(kvb.at[g, pl.ds(lo, n)], kvb.at[g, pl.ds(R1 + lo, n)], ss.at[g, i], rs.at[g, i], dev_a)

    def send_cross(g, i):
        src = (0, R1, inner + (1 - inner) * FW, inner * (R1 + 1) + (1 - inner) * (FW + 1))[i]
        return rcopy(kvb.at[g, src], kvb.at[g, CR + i], ss.at[g, 3 + i], rs.at[g, 3 + i], dev_b)

    def send_fwd(g, i):
        return rcopy(kvb.at[g, CR + i], kvb.at[g, FW + i], ss.at[g, 7 + i], rs.at[g, 7 + i], dev_a)

    def send_y(g, i):
        slot = (0, R1, ub, ub + 1, wb, wb + 1, wb + 2, wb + 3)[i]
        return rcopy(kvb.at[g, slot, pl.ds(0, 64)], r4.at[g, i], ss.at[g, 11 + i], rs.at[g, 11 + i], dev_y)

    row = lax.broadcasted_iota(i32, (ROWS, 128), 0)
    lane = lax.broadcasted_iota(i32, (ROWS, 128), 1)
    j_of = row // 64
    c_of = (j_of % 2) * 8 + (j_of // 2 % 2) * 4 + (j_of // 4 % 2) * 2 + j_of // 8
    for g in range(2):
        head = 8 * g + 4 * cc + jnp.maximum(lane - 64, 0) // 16
        posl[g] = (row % 64) * 16 + (c_of ^ head)

    rk = lax.broadcasted_iota(i32, (256, 256), 0)
    rn = lax.broadcasted_iota(i32, (256, 256), 1)
    fwd_mat = jnp.where(((rk // 16) ^ (4 * cc)) == rn % 16, jnp.where(rk % 16 == rn // 16, 1.0, 0.0), 0.0).astype(bf16)
    for q in range(4):
        t = jnp.dot(fwd_mat, x_ref[pl.ds(256 * q, 256), :], preferred_element_type=f32).astype(bf16)
        xp[:, pl.ds(16 * q, 16), :] = t.reshape(16, 16, D)

    pl.semaphore_wait(bar, 19)
    rcopy(w_ref.at[xy], wr.at[xy], w1.at[0], w1.at[1], dev_m).start()

    lane256 = lax.broadcasted_iota(i32, (1, 256), 1)
    lane_head = jnp.where(lane256 < 64, lane256 // 16, (lane256 - 64) // 48)
    q_masks = []
    for lh in range(4):
        m = jnp.where((lane256 // 48 == lh) & (lane256 < 192), 1.0, 0.0)
        q_masks.append(jnp.where(lane256 == 192 + 16 * lh, 1.0, m).astype(bf16))
    lane640 = lax.broadcasted_iota(i32, (64, 640), 1)
    head640 = lane640 % 192 // 48
    ones_lane = lane640 >= 576

    def project(g, w):
        wm = w[...].reshape(D, 640)
        for i in range(4):
            t = jnp.dot(xp[pl.ds(4 * i, 4)].reshape(256, D), wm, preferred_element_type=f32).astype(bf16)
            y[pl.ds((4 * i + 8 * g) % 16, 4)] = t.reshape(4, 64, 640)
        for j in range(16):
            c = CORD[j]
            t = y[c].astype(f32)
            for lh in range(1, 4):
                t = jnp.where(head640 == lh, y[c ^ lh].astype(f32), t)
            t = jnp.where(ones_lane, 1.0, t).astype(bf16)
            kvb[g, j // 2, pl.ds(64 * (j % 2), 64), :] = t[:, :384]
            qp[g, pl.ds(64 * j, 64), :] = t[:, 384:]

    slide = s // HALF
    count = jnp.where(slide == 0, cnt_ref[0], cnt_ref[1])

    def limit(sq):
        return count - (sq % HALF) * ROWS

    def place(g, rows, n, at, row0, sq):
        t1 = rows[:, 128:256].astype(f32)
        low = lax.broadcasted_iota(i32, (n, 128), 1) < 64
        bias = jnp.where(posl[g, pl.ds(row0, n), :] < limit(sq), 0.0, NEG)
        ka[pl.ds(at, n), 0:128] = rows[:, 0:128]
        ka[pl.ds(at, n), 128:256] = jnp.where(low, t1, bias).astype(bf16)
        va[pl.ds(at, n), 0:128] = jnp.where(low, 1.0, t1).astype(bf16)
        va[pl.ds(at, n), 128:256] = rows[:, 256:384]

    sa = s + 1 - 2 * (s % 2)
    base4 = s - s % 4
    u_src = (base4 + 2 - pair, base4 + 3 - 3 * pair)
    ob = s - zl + 4 * (1 - zl // 4)
    w_src = [ob + (3 - k) + pair * (2 * k - 3) for k in range(4)]
    to_y = 8 * (1 - 2 * (py % 2))

    def keys(g, level):
        if level == 0:
            parts = [(k, k, s) for k in range(8)]
        elif level == 1:
            parts = [(k, k, s) for k in range(4)] + [(R1 + k, k, sa) for k in range(4)]
        elif level == 2:
            parts = [(0, 0, s), (1, 1, s), (R1, 0, sa), (R1 + 1, 1, sa)]
            parts += [(ub + k, k // 2, u_src[k % 2]) for k in range(4)]
        elif level == 3:
            parts = [(0, 0, s), (R1, 0, sa), (ub, 0, u_src[0]), (ub + 1, 0, u_src[1])]
            parts += [(wb + k, 0, w_src[k]) for k in range(4)]
        else:
            srcs = [s, sa, u_src[0], u_src[1]] + w_src
            slots = [0, R1, ub, ub + 1] + [wb + k for k in range(4)]
            for i in range(8):
                place(g, kvb[g, slots[i], pl.ds(0, 64), :], 64, 64 * i, 0, srcs[i])
                place(g, r4[g, i], 64, 512 + 64 * i, 0, srcs[i] + to_y)
            return
        for i, (slot, k, sq) in enumerate(parts):
            place(g, kvb[g, slot], 128, 128 * i, 128 * k, sq)

    def attend(g, at, n, first):
        q = qp[g, pl.ds(at, n), :]
        out = jnp.zeros((n, 256), f32)
        top = jnp.zeros((n, 256), f32)
        for lh in range(4):
            sc = lax.dot_general(q * q_masks[lh], ka[...], (((1,), (1,)), ((), ())), preferred_element_type=f32)
            m = jnp.max(sc, axis=1, keepdims=True)
            wts = jnp.exp2((sc - m) * SCALE).astype(bf16)
            o = jnp.dot(wts, va[...], preferred_element_type=f32)
            out = jnp.where(lane_head == lh, o, out)
            top = jnp.where(lane_head == lh, m, top)
        if first:
            acc[g, pl.ds(at, n), :] = out
            mx[g, pl.ds(at, n), :] = top
        else:
            old = mx[g, pl.ds(at, n), :]
            new = jnp.maximum(old, top)
            a = acc[g, pl.ds(at, n), :] * jnp.exp2((old - new) * SCALE) + out * jnp.exp2((top - new) * SCALE)
            acc[g, pl.ds(at, n), :] = a
            mx[g, pl.ds(at, n), :] = new

    def when_inner(f):
        pl.when(inner == 1)(f)

    def when_outer(f):
        pl.when(inner == 0)(f)

    def phase(g, extra):
        send_l1(g, 0).start()
        send_cross(g, 0).start()
        send_l1(g, 1).start()
        keys(g, 0)

        @pl.loop(0, 4)
        def _(i):
            attend(g, pl.multiple_of(i * TILE, TILE), TILE, True)

            @pl.when(i == 0)
            def _():
                send_l1(g, 0).wait_recv()
                send_cross(g, 1).start()
                send_l1(g, 1).wait_recv()

                @when_inner
                def _():
                    send_cross(g, 2).start()
                    send_cross(g, 3).start()

                extra()

            @pl.when(i == 1)
            def _():
                @when_inner
                def _():
                    for k in range(2):
                        send_cross(g, k).wait_recv()
                        send_fwd(g, k).start()

            @pl.when(i == 2)
            def _():
                @when_outer
                def _():
                    for k in range(2):
                        send_fwd(g, k).wait_recv()
                        send_cross(g, 2 + k).start()

                send_l1(g, 2).start()

            @pl.when(i == 3)
            def _():
                @when_inner
                def _():
                    for k in range(2, 4):
                        send_cross(g, k).wait_recv()
                        send_fwd(g, k).start()

                for k in range(4):
                    send_y(g, k).start()

    def send_w(slot, k):
        return rcopy(wr.at[slot], wr.at[slot], w2s.at[k], w2r.at[slot], dev((xy + k) % 16, z, cc))

    def spread_w():
        rcopy(w_ref.at[xy], wr.at[xy], w1.at[0], w1.at[1], dev_m).wait_recv()

        @pl.loop(1, 16)
        def _(k):
            send_w(xy, k).start()

    g0, g1 = zh, 1 - zh
    project(g0, w_ref)
    phase(g0, spread_w)

    @pl.loop(1, 16)
    def _(k):
        send_w((xy + k) % 16, k).wait_recv()

    project(g1, wr)
    phase(g1, lambda: None)

    for g in range(2):
        send_l1(g, 2).wait_recv()
        keys(g, 1)

        @pl.loop(0, 2)
        def _(i):
            attend(g, pl.multiple_of(i * TILE, TILE), TILE, False)

        if g == 0:

            @when_outer
            def _():
                for gg in range(2):
                    for k in range(4):
                        send_cross(gg, k).wait_recv()
                        send_fwd(gg, k).start()
                    for k in range(2, 4):
                        send_fwd(gg, k).wait_recv()

    for g in range(2):
        keys(g, 2)
        attend(g, 0, 256, False)

    @when_inner
    def _():
        for gg in range(2):
            for k in range(4):
                send_fwd(gg, k).wait_recv()

    for gg in range(2):
        for k in range(4, 8):
            send_y(gg, k).start()
    for g in range(2):
        keys(g, 3)
        attend(g, 0, 128, False)
    for g in range(2):
        for k in range(8):
            send_y(g, k).wait_recv()
        keys(g, 4)
        attend(g, 0, 64, False)

    lim = limit(s)
    lane_t = lax.broadcasted_iota(i32, (64, 256), 1)
    hd_t = jnp.where(lane_t < 64, 4, (lane_t - 64) // 48)
    row_t = lax.broadcasted_iota(i32, (64, 256), 0)
    swap = []
    for g in range(2):

        @pl.loop(0, 16)
        def _(j):
            a = acc[g, pl.ds(pl.multiple_of(64 * j, 64), 64), :]
            den = jnp.ones((64, 256), f32)
            for lh in range(4):
                den = jnp.where(hd_t == lh, a[:, 16 * lh : 16 * lh + 1], den)
            nb[j] = jnp.where(hd_t == 4, 0.0, a / den).astype(bf16)

        for b in range(16):
            t = nb[JOF[b ^ (8 * g)]].astype(f32)
            for lh in range(1, 4):
                t = jnp.where(hd_t == lh, nb[JOF[b ^ (8 * g) ^ lh]].astype(f32), t)
            res = (b // 4 % 2 + cc) % 2 * 4 + (b - b // 4 % 2 * 4)
            att[0, g, b] = jnp.where(row_t * 16 + res < lim, t, 0.0).astype(bf16)
        cp = rcopy(att.at[0, g], att.at[1, g], cs.at[0, g], cs.at[1, g], dev_c)
        cp.start()
        swap.append(cp)

    for cp in swap:
        cp.wait_recv()
    for i in range(4):
        e = jnp.zeros((256, 192), f32)
        for g in range(2):
            own = att[0, g, pl.ds(4 * i, 4)].reshape(256, 256)
            oth = att[1, g, pl.ds(4 * (i ^ 1), 4)].reshape(256, 256)
            e += jnp.dot(own, wo_ref[2 * g + cc], preferred_element_type=f32)
            e += jnp.dot(oth, wo_ref[2 * g + 1 - cc], preferred_element_type=f32)
        eb[pl.ds(4 * i, 4)] = e.astype(bf16).reshape(4, 64, 192)
    back_mat = jnp.where(((rn // 16) ^ (4 * cc)) == rk % 16, jnp.where(rn % 16 == rk // 16, 1.0, 0.0), 0.0).astype(bf16)
    for q in range(4):
        t = eb[:, pl.ds(16 * q, 16), :].reshape(256, 192)
        o_ref[pl.ds(256 * q, 256), :] = jnp.dot(back_mat, t, preferred_element_type=f32).astype(bf16)

    rcopy(w_ref.at[xy], wr.at[xy], w1.at[0], w1.at[1], dev_m).wait_send()

    @pl.loop(1, 16)
    def _(k):
        send_w(xy, k).wait_send()

    for g in range(2):
        for k in range(3):
            send_l1(g, k).wait_send()
        for k in range(4):
            send_cross(g, k).wait_send()
            send_fwd(g, k).wait_send()
        for k in range(8):
            send_y(g, k).wait_send()
    for cp in swap:
        cp.wait_send()


def on_device(tile_embed, tile_counts, w_qkv, w_out):
    bf16, f32 = jnp.bfloat16, jnp.float32
    hd = lax.axis_index("head")
    wcat = jnp.concatenate((w_qkv[1], w_qkv[2], w_qkv[0], jnp.zeros((D, 64), bf16)), axis=1).reshape(16, 48, 640)
    cols = lax.dynamic_slice_in_dim(w_out, hd * 192, 192, 1).reshape(4, 192, 192)
    wo = jnp.pad(cols, ((0, 0), (64, 0), (0, 0)))
    vmem = pl.BlockSpec(memory_space=pltpu.VMEM)
    return pl.pallas_call(
        kernel,
        out_shape=jax.ShapeDtypeStruct((ROWS, 192), bf16),
        in_specs=[vmem, pl.BlockSpec(memory_space=pltpu.SMEM), vmem, vmem],
        out_specs=vmem,
        scratch_shapes=[
            pltpu.VMEM((16, 64, D), bf16),
            pltpu.VMEM((16, 48, 640), bf16),
            pltpu.VMEM((16, 64, 640), bf16),
            pltpu.VMEM((2, 20, 128, 384), bf16),
            pltpu.VMEM((2, 8, 64, 384), bf16),
            pltpu.VMEM((2, ROWS, 256), bf16),
            pltpu.VMEM((ROWS, 256), bf16),
            pltpu.VMEM((ROWS, 256), bf16),
            pltpu.VMEM((2, ROWS, 256), f32),
            pltpu.VMEM((2, ROWS, 256), f32),
            pltpu.VMEM((2, ROWS, 128), jnp.int32),
            pltpu.VMEM((16, 64, 256), bf16),
            pltpu.VMEM((2, 2, 16, 64, 256), bf16),
            pltpu.VMEM((16, 64, 192), bf16),
            pltpu.SemaphoreType.DMA((2, 19)),
            pltpu.SemaphoreType.DMA((2, 19)),
            pltpu.SemaphoreType.DMA((2,)),
            pltpu.SemaphoreType.DMA((16,)),
            pltpu.SemaphoreType.DMA((16,)),
            pltpu.SemaphoreType.DMA((2, 2)),
        ],
        compiler_params=pltpu.CompilerParams(
            collective_id=0, has_side_effects=True, vmem_limit_bytes=52 * 2**20
        ),
        cost_estimate=pl.CostEstimate(flops=20 * 10**9, bytes_accessed=6 * 10**6, transcendentals=17 * 10**6),
    )(tile_embed, tile_counts, wcat, wo)


def solution(mesh):
    in_specs = (P("seq", None), P(), P(None, None, "head"), P())
    out_specs = P("seq", "head")
    return jax.shard_map(
        on_device, mesh=mesh, in_specs=in_specs, out_specs=out_specs, check_vma=False
    )
```

time: 378 us -> 99.7 us (0.26)
  the two profiles are of different devices: /device:TPU:1 before, /device:TPU:47 now
where the time goes in v1:
time: 99.7 us; the launch traced here: 99.6 us
  Pallas kernels  95.1 us (95%)
  local copies, waits for them, and re-layouts  3.07 us (3%)
  other arithmetic  1.36 us (1%)
    pallas_call x1, Pallas kernels, on_device(): pl.pallas_call(kernel, out_shape=jax.ShapeDtypeStruct((ROWS, 192), bf16),...  95.1 us

profile of v1, /device:TPU:47, one launch (start us, length us, event | category | flops | bytes accessed | tf_op | source)
XLA Modules:
  0.0 99.6 jit_solution(8720211227943627831)
XLA Ops:
  0.0 0.0 copy-start
  0.0 1.3 %fusion = (bf16[1,768,192]{1,2,0:T(8,128)(2,1)S(1)}, bf16[1,768,192]{1,2,0:T(8,128)(2,1)S(1)}, bf16[1,768,192]{1,2,0:T(8,128)(2,1)S(1)}) fusion(bf16[3,768,192]{1,2,0:T(8,128)(2,1)} %param.6), kind=kLoop, calls=%fused_computation.2 | loop fusion | bytes 1769472 | tf_op jit(solution)/shard_map/slice | solution.py:364
  1.3 0.2 copy.5
  1.5 0.2 copy.6
  1.6 0.2 copy.7
  1.8 0.1 pad.8.clone
  1.9 0.0 copy-start.1
  1.9 1.4 %maximum_maximum_fusion.w_ref = bf16[16,48,640]{2,1,0:T(8,128)(2,1)} fusion(bf16[16,48,192]{2,1,0:T(8,128)(2,1)S(1)} %bitcast.6, bf16[16,48,192]{2,1,0:T(8,128)(2,1)S(1)} %bitcast.5, bf16[16,48,192]{2,1,0:T(8,128)(2,1)S(1)} %bitcast.4, bf16[640]{0:T(1024)(128)(2,1)S(1)} %pad.8.clone), kind=kLoop, calls=%fused_computation | loop fusion | flops 3932160 | bytes 1869056 | tf_op jit(solution)/shard_map/concatenate | solution.py:364
  3.3 0.0 copy-done
  3.3 0.2 constant_dynamic-slice_fusion
  3.5 0.1 pad.4.wo_ref
  3.5 0.0 copy-done.1
  3.5 95.1 %shard_map.46 = bf16[1024,192]{1,0:T(8,128)(2,1)S(1)} custom-call(bf16[1024,768]{1,0:T(8,128)(2,1)} %x_ref.1, s32[2]{0:T(128)S(1)} %copy-done.1, bf16[16,48,640]{2,1,0:T(8,128)(2,1)} %maximum_maximum_fusion.w_ref, bf16[4,256,192]{2,1,0:T(8,128)(2,1)S(1)} %pad.4.wo_ref), custom_call_target="tpu_custom_call" | custom-call | flops 20000000000 | bytes 6000000 | tf_op jit(solution)/shard_map/pallas_call | solution.py:368
  98.6 0.9 copy.8
  (1 shorter events, 0.0 us)
Async XLA Ops:
  0.0 3.3 %copy-start = (bf16[768,768]{1,0:T(8,128)(2,1)S(1)}, bf16[768,768]{1,0:T(8,128)(2,1)}, u32[]{:S(2)}) copy-start(bf16[768,768]{1,0:T(8,128)(2,1)} %param.7) | copy-start | bytes 3538948
  1.9 1.6 %copy-start.1 = (s32[2]{0:T(128)S(1)}, s32[2]{0:T(128)}, u32[]{:S(2)}) copy-start(s32[2]{0:T(128)} %cnt_ref.1) | copy-start | bytes 28

commit v2 on v1

v2 whole, which is shorter than its diff:
```python
import functools
import math

import jax
import jax.numpy as jnp
from jax import lax
from jax.experimental import pallas as pl
from jax.experimental.pallas import tpu as pltpu
from jax.sharding import PartitionSpec as P

HD = 48
ROWS = 1024
D = 768
HALF = 64
CORD = [int(f"{j:04b}"[::-1], 2) for j in range(16)]
JOF = [CORD.index(c) for c in range(16)]
NEG = -1e30
SCALE = math.log2(math.e) / math.sqrt(HD)
MESH = pl.DeviceIdType.MESH
TILE = 256

R1, US, WS = 8, 12, 16


def kernel(x_ref, cnt_ref, wq_ref, wout_ref, o_ref, w_ref, wo_ref, xp, wr, y, kvb, r4, qp, ka, va, acc, mx, posl, nb, att, eb,
           ss, rs, w1, w2s, w2r, cs):
    f32, bf16, i32 = jnp.float32, jnp.bfloat16, jnp.int32
    s = lax.axis_index("seq")
    hd = lax.axis_index("head")
    px, py, zl = s // 32, s // 8 % 4, s % 8
    zh, cc = hd // 2, hd % 2
    z = zh * 8 + zl
    xy = px * 4 + py
    p4 = zl % 4
    pair = p4 // 2
    inner = (p4 + 1) // 2 % 2
    za = z + 1 - 2 * (z % 2)
    zb = (z + 15 + 2 * (z % 2)) % 16
    zw = (8 * zh + 15 - 7 * (zl // 4)) % 16
    edge = 1 - (zl + 6) // 7 + zl // 7
    zd = (8 * zh + 15 - 7 * (zl // 7)) % 16
    step = 1 - 2 * (1 - zl // 7)
    za_b = (za + 15 + 2 * (za % 2)) % 16
    zh_w = (inner * za_b + (1 - inner) * zb) // 8
    zf = z + 2 - 4 * pair

    def dev(xy_, z_, c_):
        return (xy_ * 8 + z_ % 8, z_ // 8 * 2 + c_)

    dev_a, dev_b, dev_w, dev_c = dev(xy, za, cc), dev(xy, zb, cc), dev(xy, zw, cc), dev(xy, z, 1 - cc)
    dev_f = dev(xy, zf, cc)
    dev_y = dev(xy + 1 - 2 * (py % 2), z, cc)

    bar = pltpu.get_barrier_semaphore()
    for d in (dev_a, dev_b, dev_w, dev_c, dev_f):
        pl.semaphore_signal(bar, inc=1, device_id=d, device_id_type=MESH)

    @pl.loop(1, 16)
    def _(k):
        pl.semaphore_signal(bar, inc=1, device_id=dev((xy + k) % 16, z, cc), device_id_type=MESH)

    def rcopy(src, dst, ssem, rsem, d):
        return pltpu.make_async_remote_copy(
            src_ref=src, dst_ref=dst, send_sem=ssem, recv_sem=rsem, device_id=d, device_id_type=MESH
        )

    def send_l1(g, i):
        lo, n = ((0, 1), (1, 1), (2, 2))[i]
        return rcopy(kvb.at[g, pl.ds(lo, n)], kvb.at[g, pl.ds(R1 + lo, n)], ss.at[g, i], rs.at[g, i], dev_a)

    def send_u(g, i, k):
        src, dst = ((0, US), (R1, US + 2))[i]
        return rcopy(kvb.at[g, pl.ds(src, 2)], kvb.at[g, pl.ds(dst, 2)], ss.at[g, 3 + 2 * i + k], rs.at[g, 3 + i],
                     (dev_b, dev_f)[k])

    def send_cross(g, i):
        src = (0, R1, US, US + 2)[i]
        return rcopy(kvb.at[g, src], kvb.at[g, WS + i], ss.at[g, 7 + i], rs.at[g, 7 + i], dev_b)

    def send_fwd(g, i):
        return rcopy(kvb.at[g, WS + i], kvb.at[g, WS + i], ss.at[g, 19 + i], rs.at[g, 7 + i], dev_a)

    def send_y(g, i):
        slot = (0, R1, US, US + 2, WS, WS + 1, WS + 2, WS + 3)[i]
        return rcopy(kvb.at[g, slot, pl.ds(0, 64)], r4.at[g, i], ss.at[g, 11 + i], rs.at[g, 11 + i], dev_y)

    for k in range(16):
        rows = pl.ds(48 * k, 48)
        parts = (wq_ref[1, rows, :], wq_ref[2, rows, :], wq_ref[0, rows, :], jnp.zeros((48, 64), bf16))
        w_ref[k] = jnp.concatenate(parts, axis=1)
    for k in range(4):

        @pl.when(hd == k)
        def _():
            for i in range(4):
                wo_ref[i, 0:64, :] = jnp.zeros((64, 192), bf16)
                wo_ref[i, 64:256, :] = wout_ref[pl.ds(192 * i, 192), 192 * k : 192 * k + 192]

    row = lax.broadcasted_iota(i32, (ROWS, 128), 0)
    lane = lax.broadcasted_iota(i32, (ROWS, 128), 1)
    j_of = row // 64
    c_of = (j_of % 2) * 8 + (j_of // 2 % 2) * 4 + (j_of // 4 % 2) * 2 + j_of // 8
    for g in range(2):
        head = 8 * g + 4 * cc + jnp.maximum(lane - 64, 0) // 16
        posl[g] = (row % 64) * 16 + (c_of ^ head)

    rk = lax.broadcasted_iota(i32, (256, 256), 0)
    rn = lax.broadcasted_iota(i32, (256, 256), 1)
    fwd_mat = jnp.where(((rk // 16) ^ (4 * cc)) == rn % 16, jnp.where(rk % 16 == rn // 16, 1.0, 0.0), 0.0).astype(bf16)
    for q in range(4):
        t = jnp.dot(fwd_mat, x_ref[pl.ds(256 * q, 256), :], preferred_element_type=f32).astype(bf16)
        xp[:, pl.ds(16 * q, 16), :] = t.reshape(16, 16, D)

    lane256 = lax.broadcasted_iota(i32, (1, 256), 1)
    lane_head = jnp.where(lane256 < 64, lane256 // 16, (lane256 - 64) // 48)
    q_head = jnp.where(lane256 < 192, lane256 // 48, jnp.where(lane256 % 16 == 0, (lane256 - 192) // 16, 4))
    lane640 = lax.broadcasted_iota(i32, (64, 640), 1)
    head640 = lane640 % 192 // 48
    ones_lane = lane640 >= 576

    def project(g, w, lo, n):
        wm = w[:, :, lo : lo + n].reshape(D, n)
        for i in range(4):
            t = jnp.dot(xp[pl.ds(4 * i, 4)].reshape(256, D), wm, preferred_element_type=f32).astype(bf16)
            y[pl.ds((4 * i + 8 * g) % 16, 4), :, lo : lo + n] = t.reshape(4, 64, n)
        for j in range(16):
            c = CORD[j]
            t = y[c, :, lo : lo + n].astype(f32)
            for lh in range(1, 4):
                t = jnp.where(head640[:, lo : lo + n] == lh, y[c ^ lh, :, lo : lo + n].astype(f32), t)
            if lo == 0:
                kvb[g, j // 2, pl.ds(64 * (j % 2), 64), :] = t.astype(bf16)
            else:
                t = jnp.where(ones_lane[:, lo : lo + n], 1.0, t).astype(bf16)
                qp[g, pl.ds(64 * j, 64), :] = t

    slide = s // HALF
    count = jnp.where(slide == 0, cnt_ref[0], cnt_ref[1])

    def limit(sq):
        return count - (sq % HALF) * ROWS

    def place(g, rows, n, at, row0, sq):
        t1 = rows[:, 128:256].astype(f32)
        low = lax.broadcasted_iota(i32, (n, 128), 1) < 64
        bias = jnp.where(posl[g, pl.ds(row0, n), :] < limit(sq), 0.0, NEG)
        ka[pl.ds(at, n), 0:128] = rows[:, 0:128]
        ka[pl.ds(at, n), 128:256] = jnp.where(low, t1, bias).astype(bf16)
        va[pl.ds(at, n), 0:128] = jnp.where(low, 1.0, t1).astype(bf16)
        va[pl.ds(at, n), 128:256] = rows[:, 256:384]

    sa = s + 1 - 2 * (s % 2)
    base4 = s - s % 4
    u_src = (base4 + 2 - pair, base4 + 3 - 3 * pair)
    ob = s - zl + 4 * (1 - zl // 4)
    w_src = [ob + (3 - k) + pair * (2 * k - 3) for k in range(4)]
    to_y = 8 * (1 - 2 * (py % 2))

    def keys(g, level):
        if level == 0:
            parts = [(k, k, s) for k in range(8)]
        elif level == 1:
            parts = [(k, k, s) for k in range(4)] + [(R1 + k, k, sa) for k in range(4)]
        elif level == 2:
            parts = [(0, 0, s), (1, 1, s), (R1, 0, sa), (R1 + 1, 1, sa)]
            parts += [(US + k, k % 2, u_src[k // 2]) for k in range(4)]
        elif level == 3:
            parts = [(0, 0, s), (R1, 0, sa), (US, 0, u_src[0]), (US + 2, 0, u_src[1])]
            parts += [(WS + k, 0, w_src[k]) for k in range(4)]
        else:
            srcs = [s, sa, u_src[0], u_src[1]] + w_src
            slots = [0, R1, US, US + 2] + [WS + k for k in range(4)]
            for i in range(8):
                place(g, kvb[g, slots[i], pl.ds(0, 64), :], 64, 64 * i, 0, srcs[i])
                place(g, r4[g, i], 64, 512 + 64 * i, 0, srcs[i] + to_y)
            return
        for i, (slot, k, sq) in enumerate(parts):
            place(g, kvb[g, slot], 128, 128 * i, 128 * k, sq)

    def attend(g, at, n, first):
        rows = pl.ds(at, n)
        q = qp[g, rows, :]
        out = jnp.zeros((n, 256), f32)
        top = jnp.zeros((n, 256), f32)
        for lh in range(4):
            qh = q * jnp.where(q_head == lh, 1.0, 0.0).astype(bf16)
            sc = lax.dot_general(qh, ka[...], (((1,), (1,)), ((), ())), preferred_element_type=f32)
            m = jnp.max(sc, axis=1, keepdims=True)
            wts = jnp.exp2((sc - m) * SCALE).astype(bf16)
            o = jnp.dot(wts, va[...], preferred_element_type=f32)
            out = jnp.where(lane_head == lh, o, out)
            top = jnp.where(lane_head == lh, m, top)
        if first:
            acc[g, rows, :] = out
            mx[g, rows, :] = top
        else:
            old = mx[g, rows, :]
            new = jnp.maximum(old, top)
            acc[g, rows, :] = acc[g, rows, :] * jnp.exp2((old - new) * SCALE) + out * jnp.exp2((top - new) * SCALE)
            mx[g, rows, :] = new

    def when_inner(f):
        pl.when(inner == 1)(f)

    def when_outer(f):
        pl.when(inner == 0)(f)

    def start_w(part):
        @pl.when(edge == 1)
        def _():
            @pl.loop(0, 4)
            def _(k):
                copy_w(part, k, dev(xy, (zd + k * step + 16) % 16, cc)).start()

    def copy_w(part, k, d):
        lanes = pl.ds(384 * part, 384 - 128 * part)
        return rcopy(w_ref.at[xy, :, lanes], wr.at[xy, :, lanes], w1.at[part, k], w1.at[part, 4], d)

    def send_w(part, slot, k):
        lanes = pl.ds(384 * part, 384 - 128 * part)
        ref = wr.at[slot, :, lanes]
        return rcopy(ref, ref, w2s.at[part, k], w2r.at[part, slot], dev((xy + k) % 16, z, cc))

    def spread_w(part):
        copy_w(part, 0, dev_w).wait_recv()

        @pl.loop(1, 16)
        def _(k):
            send_w(part, xy, k).start()

    def wait_w(part):
        @pl.loop(1, 16)
        def _(k):
            send_w(part, (xy + k) % 16, k).wait_recv()

    def s1(g):
        send_l1(g, 0).start()

        @when_inner
        def _():
            send_u(g, 0, 1).start()
            send_u(g, 0, 0).start()

        @when_outer
        def _():
            send_cross(g, 0).start()

        send_l1(g, 1).start()
        send_y(g, 0).start()

    def s2(g):
        send_l1(g, 0).wait_recv()
        send_l1(g, 1).wait_recv()

        @when_inner
        def _():
            send_u(g, 1, 1).start()
            send_u(g, 1, 0).start()

        @when_outer
        def _():
            send_cross(g, 1).start()

        send_l1(g, 2).start()
        send_y(g, 1).start()

    def s3(g):
        for i in range(2):
            send_u(g, i, 0).wait_recv()

            @when_outer
            def _():
                send_cross(g, 2 + i).start()

            send_y(g, 2 + i).start()

    def s4(g):
        @when_outer
        def _():
            for k in range(4):
                send_cross(g, k).wait_recv()
                send_fwd(g, k).start()
                send_y(g, 4 + k).start()


    def s5(g):
        @when_inner
        def _():
            for k in range(4):
                send_fwd(g, k).wait_recv()
                send_y(g, 4 + k).start()

    def local(g, steps):
        @pl.loop(0, 4)
        def _(i):
            attend(g, pl.multiple_of(i * TILE, TILE), TILE, True)
            for k, step in steps.items():
                pl.when(i == k)(step)

    def level(g, lv):
        keys(g, lv)
        n = ROWS >> lv

        @pl.loop(0, max(n // TILE, 1))
        def _(i):
            attend(g, pl.multiple_of(i * TILE, TILE), min(n, TILE), False)

    g0, g1 = zh, 1 - zh
    gw0, gw1 = zh_w, 1 - zh_w
    project(g0, w_ref, 0, 384)
    project(g0, w_ref, 384, 256)
    pl.semaphore_wait(bar, 19 + 4 * edge)
    start_w(0)
    s1(g0)
    start_w(1)
    keys(g0, 0)

    def step0():
        s2(g0)

    def step1():
        spread_w(0)

    def step2():
        s3(g0)
        spread_w(1)

    local(g0, {0: step0, 1: step1, 2: step2})
    wait_w(0)
    project(g1, wr, 0, 384)
    s1(g1)
    s4(gw0)
    wait_w(1)
    project(g1, wr, 384, 256)
    keys(g1, 0)

    def step4():
        s2(g1)
        s5(gw0)

    def step5():
        s3(g1)

    local(g1, {0: step4, 2: step5})
    level(g0, 2)
    s4(gw1)
    send_l1(g0, 2).wait_recv()
    level(g0, 1)
    s5(gw1)
    level(g1, 2)
    send_l1(g1, 2).wait_recv()
    level(g1, 1)
    for g in (g0, g1):
        level(g, 3)
    for g in (g0, g1):
        for k in range(8):
            send_y(g, k).wait_recv()
        level(g, 4)

    lim = limit(s)
    lane_t = lax.broadcasted_iota(i32, (64, 256), 1)
    hd_t = jnp.where(lane_t < 64, 4, (lane_t - 64) // 48)
    row_t = lax.broadcasted_iota(i32, (64, 256), 0)
    swap = []
    for g in range(2):

        @pl.loop(0, 16)
        def _(j):
            a = acc[g, pl.ds(pl.multiple_of(64 * j, 64), 64), :]
            den = jnp.ones((64, 256), f32)
            for lh in range(4):
                den = jnp.where(hd_t == lh, a[:, 16 * lh : 16 * lh + 1], den)
            nb[j] = jnp.where(hd_t == 4, 0.0, a / den).astype(bf16)

        for b in range(16):
            t = nb[JOF[b ^ (8 * g)]].astype(f32)
            for lh in range(1, 4):
                t = jnp.where(hd_t == lh, nb[JOF[b ^ (8 * g) ^ lh]].astype(f32), t)
            res = (b // 4 % 2 + cc) % 2 * 4 + (b - b // 4 % 2 * 4)
            att[0, g, b] = jnp.where(row_t * 16 + res < lim, t, 0.0).astype(bf16)
        cp = rcopy(att.at[0, g], att.at[1, g], cs.at[0, g], cs.at[1, g], dev_c)
        cp.start()
        swap.append(cp)

    for cp in swap:
        cp.wait_recv()
    for i in range(4):
        e = jnp.zeros((256, 192), f32)
        for g in range(2):
            own = att[0, g, pl.ds(4 * i, 4)].reshape(256, 256)
            oth = att[1, g, pl.ds(4 * (i ^ 1), 4)].reshape(256, 256)
            e += jnp.dot(own, wo_ref[2 * g + cc], preferred_element_type=f32)
            e += jnp.dot(oth, wo_ref[2 * g + 1 - cc], preferred_element_type=f32)
        eb[pl.ds(4 * i, 4)] = e.astype(bf16).reshape(4, 64, 192)
    back_mat = jnp.where(((rn // 16) ^ (4 * cc)) == rk % 16, jnp.where(rn % 16 == rk // 16, 1.0, 0.0), 0.0).astype(bf16)
    for q in range(4):
        t = eb[:, pl.ds(16 * q, 16), :].reshape(256, 192)
        o_ref[pl.ds(256 * q, 256), :] = jnp.dot(back_mat, t, preferred_element_type=f32).astype(bf16)

    for part in range(2):

        @pl.when(edge == 1)
        def _():
            @pl.loop(0, 4)
            def _(k):
                copy_w(part, k, dev_w).wait_send()

        @pl.loop(1, 16)
        def _(k):
            send_w(part, xy, k).wait_send()

    for g in range(2):
        for k in range(3):
            send_l1(g, k).wait_send()

        @when_inner
        def _():
            for i in range(2):
                for k in range(2):
                    send_u(g, i, k).wait_send()

        @when_outer
        def _():
            for k in range(4):
                send_cross(g, k).wait_send()
                send_fwd(g, k).wait_send()

        for k in range(8):
            send_y(g, k).wait_send()
    for cp in swap:
        cp.wait_send()


def on_device(tile_embed, tile_counts, w_qkv, w_out):
    bf16, f32 = jnp.bfloat16, jnp.float32
    vmem = pl.BlockSpec(memory_space=pltpu.VMEM)
    return pl.pallas_call(
        kernel,
        out_shape=jax.ShapeDtypeStruct((ROWS, 192), bf16),
        in_specs=[vmem, pl.BlockSpec(memory_space=pltpu.SMEM), vmem, vmem],
        out_specs=vmem,
        scratch_shapes=[
            pltpu.VMEM((16, 48, 640), bf16),
            pltpu.VMEM((4, 256, 192), bf16),
            pltpu.VMEM((16, 64, D), bf16),
            pltpu.VMEM((16, 48, 640), bf16),
            pltpu.VMEM((16, 64, 640), bf16),
            pltpu.VMEM((2, 20, 128, 384), bf16),
            pltpu.VMEM((2, 8, 64, 384), bf16),
            pltpu.VMEM((2, ROWS, 256), bf16),
            pltpu.VMEM((ROWS, 256), bf16),
            pltpu.VMEM((ROWS, 256), bf16),
            pltpu.VMEM((2, ROWS, 256), f32),
            pltpu.VMEM((2, ROWS, 256), f32),
            pltpu.VMEM((2, ROWS, 128), jnp.int32),
            pltpu.VMEM((16, 64, 256), bf16),
            pltpu.VMEM((2, 2, 16, 64, 256), bf16),
            pltpu.VMEM((16, 64, 192), bf16),
            pltpu.SemaphoreType.DMA((2, 23)),
            pltpu.SemaphoreType.DMA((2, 19)),
            pltpu.SemaphoreType.DMA((2, 5)),
            pltpu.SemaphoreType.DMA((2, 16)),
            pltpu.SemaphoreType.DMA((2, 16)),
            pltpu.SemaphoreType.DMA((2, 2)),
        ],
        compiler_params=pltpu.CompilerParams(
            collective_id=0, has_side_effects=True, vmem_limit_bytes=52 * 2**20
        ),
        cost_estimate=pl.CostEstimate(flops=20 * 10**9, bytes_accessed=6 * 10**6, transcendentals=17 * 10**6),
    )(tile_embed, tile_counts, w_qkv, w_out)


def solution(mesh):
    in_specs = (P("seq", None), P(), P(None, None, "head"), P())
    out_specs = P("seq", "head")
    return jax.shard_map(
        on_device, mesh=mesh, in_specs=in_specs, out_specs=out_specs, check_vma=False
    )
```

time: 99.7 us -> 90.2 us (0.905)
  the two profiles are of different devices: /device:TPU:47 before, /device:TPU:1 now
where the time goes in v2:
time: 90.2 us; the launch traced here: 90 us
  Pallas kernels  87.5 us (97%)
  local copies, waits for them, and re-layouts  2.47 us (3%)
    pallas_call x1, Pallas kernels, on_device(): pl.pallas_call(kernel, out_shape=jax.ShapeDtypeStruct((ROWS, 192), bf16),...  87.5 us

profile of v2, /device:TPU:1, one launch (start us, length us, event | category | flops | bytes accessed | tf_op | source)
XLA Modules:
  0.0 90.0 jit_solution(2255674079541785500)
XLA Ops:
  0.0 0.0 copy-start
  0.0 1.5 %copy.5.wq_ref = bf16[3,768,192]{2,1,0:T(8,128)(2,1)S(1)} copy(bf16[3,768,192]{1,2,0:T(8,128)(2,1)} %param.6) | data formatting | bytes 1769472 | tf_op args[2]
  1.5 0.0 copy-done
  1.5 87.5 %shard_map.46 = bf16[1024,192]{1,0:T(8,128)(2,1)S(1)} custom-call(bf16[1024,768]{1,0:T(8,128)(2,1)} %x_ref.1, s32[2]{0:T(128)S(1)} %copy-done, bf16[3,768,192]{2,1,0:T(8,128)(2,1)S(1)} %copy.5.wq_ref, bf16[768,768]{1,0:T(8,128)(2,1)} %wout_ref.1), custom_call_target="tpu_custom_call" | custom-call | flops 20000000000 | bytes 6000000 | tf_op jit(solution)/shard_map/pallas_call | solution.py:437
  89.1 0.9 %copy.6 = bf16[1024,192]{0,1:T(8,128)(2,1)} copy(bf16[1024,192]{1,0:T(8,128)(2,1)S(1)} %shard_map.46) | data formatting | bytes 786432 | tf_op jit(solution)/shard_map/pallas_call | solution.py:437
Async XLA Ops:
  0.0 1.5 %copy-start = (s32[2]{0:T(128)S(1)}, s32[2]{0:T(128)}, u32[]{:S(2)}) copy-start(s32[2]{0:T(128)} %cnt_ref.1) | copy-start | bytes 28

commit v3 on v2

--- a/solution.py
+++ b/solution.py
@@ -317,37 +317,39 @@
 
     def step0():
         s2(g0)
+        spread_w(0)
 
     def step1():
-        spread_w(0)
+        spread_w(1)
 
     def step2():
         s3(g0)
-        spread_w(1)
 
     local(g0, {0: step0, 1: step1, 2: step2})
+    level(g0, 2)
+    s4(gw0)
     wait_w(0)
     project(g1, wr, 0, 384)
     s1(g1)
-    s4(gw0)
+    send_l1(g0, 2).wait_recv()
+    keys(g0, 1)
+    attend(g0, 0, 256, False)
+    s2(g1)
+    s5(gw0)
+    attend(g0, 256, 256, False)
     wait_w(1)
     project(g1, wr, 384, 256)
     keys(g1, 0)
 
+    def step3():
+        s3(g1)
+
     def step4():
-        s2(g1)
-        s5(gw0)
-
-    def step5():
-        s3(g1)
-
-    local(g1, {0: step4, 2: step5})
-    level(g0, 2)
-    s4(gw1)
-    send_l1(g0, 2).wait_recv()
-    level(g0, 1)
+        s4(gw1)
+
+    local(g1, {0: step3, 2: step4})
+    level(g1, 2)
     s5(gw1)
-    level(g1, 2)
     send_l1(g1, 2).wait_recv()
     level(g1, 1)
     for g in (g0, g1):

time: 90.2 us -> 90.5 us (level)
  no operation moved by 1% of the time
where the time goes in v3:
time: 90.5 us; the launch traced here: 90.4 us
  Pallas kernels  87.9 us (97%)
  local copies, waits for them, and re-layouts  2.47 us (3%)
    pallas_call x1, Pallas kernels, on_device(): pl.pallas_call(kernel, out_shape=jax.ShapeDtypeStruct((ROWS, 192), bf16),...  87.9 us

profile of v3, /device:TPU:1, one launch (start us, length us, event | category | flops | bytes accessed | tf_op | source)
XLA Modules:
  0.0 90.4 jit_solution(11116533615245561246)
XLA Ops:
  0.0 0.0 copy-start
  0.0 1.5 %copy.5.wq_ref = bf16[3,768,192]{2,1,0:T(8,128)(2,1)S(1)} copy(bf16[3,768,192]{1,2,0:T(8,128)(2,1)} %param.6) | data formatting | bytes 1769472 | tf_op args[2]
  1.5 0.0 copy-done
  1.5 87.9 %shard_map.46 = bf16[1024,192]{1,0:T(8,128)(2,1)S(1)} custom-call(bf16[1024,768]{1,0:T(8,128)(2,1)} %x_ref.1, s32[2]{0:T(128)S(1)} %copy-done, bf16[3,768,192]{2,1,0:T(8,128)(2,1)S(1)} %copy.5.wq_ref, bf16[768,768]{1,0:T(8,128)(2,1)} %wout_ref.1), custom_call_target="tpu_custom_call" | custom-call | flops 20000000000 | bytes 6000000 | tf_op jit(solution)/shard_map/pallas_call | solution.py:439
  89.4 0.9 %copy.6 = bf16[1024,192]{0,1:T(8,128)(2,1)} copy(bf16[1024,192]{1,0:T(8,128)(2,1)S(1)} %shard_map.46) | data formatting | bytes 786432 | tf_op jit(solution)/shard_map/pallas_call | solution.py:439
Async XLA Ops:
  0.0 1.5 %copy-start = (s32[2]{0:T(128)S(1)}, s32[2]{0:T(128)}, u32[]{:S(2)}) copy-start(s32[2]{0:T(128)} %cnt_ref.1) | copy-start | bytes 28

commit v4 on v3

--- a/solution.py
+++ b/solution.py
@@ -300,10 +300,7 @@
     def level(g, lv):
         keys(g, lv)
         n = ROWS >> lv
-
-        @pl.loop(0, max(n // TILE, 1))
-        def _(i):
-            attend(g, pl.multiple_of(i * TILE, TILE), min(n, TILE), False)
+        attend(g, 0, n, False)
 
     g0, g1 = zh, 1 - zh
     gw0, gw1 = zh_w, 1 - zh_w

time: 90.5 us -> 89.5 us (0.989)
  Pallas kernels: 87.9 us -> 86.9 us
    pallas_call x1, Pallas kernels: 87.9 us -> 86.9 us  [on_device(): pl.pallas_call(kernel, out_shape=jax.ShapeDtypeStruct((ROWS, 192), bf16),...]
where the time goes in v4:
time: 89.5 us; the launch traced here: 89.4 us
  Pallas kernels  86.9 us (97%)
  local copies, waits for them, and re-layouts  2.47 us (3%)
    pallas_call x1, Pallas kernels, on_device(): pl.pallas_call(kernel, out_shape=jax.ShapeDtypeStruct((ROWS, 192), bf16),...  86.9 us

profile of v4, /device:TPU:1, one launch (start us, length us, event | category | flops | bytes accessed | tf_op | source)
XLA Modules:
  0.0 89.4 jit_solution(11441039814816996578)
XLA Ops:
  0.0 0.0 copy-start
  0.0 1.5 %copy.5.wq_ref = bf16[3,768,192]{2,1,0:T(8,128)(2,1)S(1)} copy(bf16[3,768,192]{1,2,0:T(8,128)(2,1)} %param.6) | data formatting | bytes 1769472 | tf_op args[2]
  1.5 0.0 copy-done
  1.5 86.9 %shard_map.46 = bf16[1024,192]{1,0:T(8,128)(2,1)S(1)} custom-call(bf16[1024,768]{1,0:T(8,128)(2,1)} %x_ref.1, s32[2]{0:T(128)S(1)} %copy-done, bf16[3,768,192]{2,1,0:T(8,128)(2,1)S(1)} %copy.5.wq_ref, bf16[768,768]{1,0:T(8,128)(2,1)} %wout_ref.1), custom_call_target="tpu_custom_call" | custom-call | flops 20000000000 | bytes 6000000 | tf_op jit(solution)/shard_map/pallas_call | solution.py:436
  88.4 0.9 %copy.6 = bf16[1024,192]{0,1:T(8,128)(2,1)} copy(bf16[1024,192]{1,0:T(8,128)(2,1)S(1)} %shard_map.46) | data formatting | bytes 786432 | tf_op jit(solution)/shard_map/pallas_call | solution.py:436
Async XLA Ops:
  0.0 1.5 %copy-start = (s32[2]{0:T(128)S(1)}, s32[2]{0:T(128)}, u32[]{:S(2)}) copy-start(s32[2]{0:T(128)} %cnt_ref.1) | copy-start | bytes 28
